TPU v7x, 512 devices: a whole 4x8x8 slice. The times are simulated.
512 devices in a mesh: dp: 128 (over y, z, core), sub: 4 (over x).
Axes of the slice: x: 4, y: 8, z: 8, core: 2. Of those that a mesh axis runs over, the one named last changes fastest.
Arguments:
- tokens: bfloat16 [256, 7168], P('dp', 'sub'), may hold values from -10.5 to 10.5
- new_tokens: int32 [128], P('dp'), may hold values from 1 to 2, as said below
- dense_gain: float32 [7168], P('sub'), may hold values from 0.25 to 1.75
- dense_gate: bfloat16 [7168, 18432], P('sub', 'dp'), may hold values from -0.0625 to 0.0625
- dense_up: bfloat16 [7168, 18432], P('sub', 'dp'), may hold values from -0.0625 to 0.0625
- dense_down: bfloat16 [18432, 7168], P('dp', 'sub'), may hold values from -0.046875 to 0.046875
- moe_gain: float32 [7168], P('sub'), may hold values from 0.25 to 1.75
- expert_ids: int32 [256, 8], P('dp'), may hold values from 0 to 15, all different within a row; in each aligned block of 2 rows (0 to 1, 2 to 3, ...) at most 2 rows name the same one
- expert_weights: float32 [256, 8], P('dp'), may hold values from 0.1 to 1
- expert_gate: bfloat16 [7168, 32768], P('sub', 'dp'), may hold values from -0.0625 to 0.0625
- expert_up: bfloat16 [7168, 32768], P('sub', 'dp'), may hold values from -0.0625 to 0.0625
- expert_down: bfloat16 [32768, 7168], P('dp', 'sub'), may hold values from -0.125 to 0.125
Outputs:
- result: bfloat16 [256, 7168], P('dp', 'sub')
Inputs may be any that keep to these rules, and one draw needn't show every extreme that they name: `new_tokens`: some request group is full in every draw. `expert_ids`: each row names 8 different experts. Among the 2 rows of one request group no expert is named by more than 2 rows, and in every draw some expert is named by exactly 2 rows of some group.
All inputs are finite; a program needn't handle non-finite values.
Results may differ from a plain program's by a relative error of at most 0.022.
Values may be sent and summed in bfloat16 or wider, within the bound.
A program may use at most 64 MiB of HBM per device.

v0:
```python
import jax
import jax.numpy as jnp
from jax import lax
from jax.sharding import PartitionSpec as P

D = 7168
EH = 2048
EXPERTS = 16
CAP = 2


def normalize(stream, totals, gain_vector):
    scale_factor = lax.rsqrt(totals / D + 1e-06)
    return (stream * scale_factor[:, None] * gain_vector[None, :]).astype(jnp.bfloat16)


def routed_mask(route_ids, first_expert, expert_span):
    offset = route_ids - first_expert
    return jnp.any((offset >= 0) & (offset < expert_span), axis=-1)


def slot_choice(routed, slot_count):
    routed_count = routed.astype(jnp.int32)
    slot_rank = jnp.cumsum(routed_count, axis=1) - routed_count
    slot_places = jnp.arange(slot_count, dtype=jnp.int32)
    return routed[:, None, :] & (slot_rank[:, None, :] == slot_places[None, :, None])


def shards(
    tokens,
    new_tokens,
    dense_gain,
    dense_gate,
    dense_up,
    dense_down,
    moe_gain,
    expert_ids,
    expert_weights,
    expert_gate,
    expert_up,
    expert_down,
):
    local_rows = tokens.shape[0]
    peer_count = lax.axis_size("dp")
    token_stream = tokens.astype(jnp.float32)
    totals = lax.psum(jnp.sum(token_stream * token_stream, axis=1), "sub")
    dense_normed = normalize(token_stream, totals, dense_gain)
    row_piece = lax.all_gather(dense_normed, "dp", axis=0, tiled=True)
    stacked = jnp.stack(
        (
            jnp.dot(row_piece, dense_gate, preferred_element_type=jnp.float32),
            jnp.dot(row_piece, dense_up, preferred_element_type=jnp.float32),
        )
    )
    gate_up = lax.psum(stacked.astype(jnp.bfloat16), "sub").astype(jnp.float32)
    dense_hidden = (jax.nn.silu(gate_up[0]) * gate_up[1]).astype(jnp.bfloat16)
    dense_sum = lax.psum_scatter(
        jnp.dot(dense_hidden, dense_down, preferred_element_type=jnp.float32),
        "dp",
        scatter_dimension=0,
        tiled=True,
    )
    mixed_stream = (token_stream + dense_sum).astype(jnp.bfloat16)
    moe_stream = mixed_stream.astype(jnp.float32)
    moe_totals = lax.psum(jnp.sum(moe_stream * moe_stream, axis=1), "sub")
    moe_normed = normalize(moe_stream, moe_totals, moe_gain)
    local_cols = expert_gate.shape[1]
    expert_span = max(1, local_cols // EH)
    part_width = local_cols // expert_span
    slot_count = min(local_rows, CAP * expert_span)
    peer_first = jnp.arange(peer_count, dtype=jnp.int32) * local_cols // EH
    sending = slot_choice(
        routed_mask(expert_ids[None, :, :], peer_first[:, None, None], expert_span), slot_count
    )
    outgoing = jnp.einsum(
        "psr,rd->psd", sending.astype(jnp.bfloat16), moe_normed, preferred_element_type=jnp.float32
    ).astype(jnp.bfloat16)
    arrived = lax.all_to_all(outgoing, "dp", split_axis=0, concat_axis=0, tiled=True)
    flat_rows = arrived.reshape(peer_count * slot_count, -1)
    expert_gate_up = lax.psum(
        jnp.stack(
            (
                jnp.dot(flat_rows, expert_gate, preferred_element_type=jnp.float32),
                jnp.dot(flat_rows, expert_up, preferred_element_type=jnp.float32),
            )
        ).astype(jnp.bfloat16),
        "sub",
    ).astype(jnp.float32)
    expert_hidden = (jax.nn.silu(expert_gate_up[0]) * expert_gate_up[1]).astype(jnp.bfloat16)
    partial_value = jnp.einsum(
        "nkh,khd->nkd",
        expert_hidden.reshape(-1, expert_span, part_width),
        expert_down.reshape(expert_span, part_width, -1),
        preferred_element_type=jnp.float32,
    )
    returned = lax.all_to_all(
        partial_value.reshape(peer_count, slot_count * expert_span, -1).astype(jnp.bfloat16),
        "dp",
        split_axis=0,
        concat_axis=0,
        tiled=True,
    ).astype(jnp.float32)
    labels = jnp.arange(EXPERTS, dtype=jnp.int32)
    combine = jnp.sum(
        expert_weights[:, :, None]
        * (expert_ids[:, :, None] == labels[None, None, :]).astype(jnp.float32),
        axis=1,
    )
    span_index = jnp.arange(expert_span, dtype=jnp.int32)
    expert_pick = (
        (peer_first[:, None] + span_index[None, :])[:, :, None] == labels[None, None, :]
    ).astype(jnp.float32)
    peer_weight = jnp.einsum("re,pje->rpj", combine, expert_pick, precision=lax.Precision.HIGHEST)
    mixing = (
        jnp.transpose(sending.astype(jnp.float32), (2, 0, 1))[:, :, :, None]
        * peer_weight[:, :, None, :]
    )
    moe_sum = jnp.dot(
        mixing.reshape(local_rows, -1),
        returned.reshape(-1, returned.shape[2]),
        precision=lax.Precision.HIGHEST,
        preferred_element_type=jnp.float32,
    )
    running_total = moe_stream + moe_sum
    live_slots = jnp.arange(local_rows, dtype=jnp.int32) < new_tokens[0]
    return jnp.where(live_slots[:, None], running_total, 0.0).astype(jnp.bfloat16)


def solution(mesh):
    placed = (
        P("dp", "sub"),
        P("dp"),
        P("sub"),
        P("sub", "dp"),
        P("sub", "dp"),
        P("dp", "sub"),
        P("sub"),
        P("dp", None),
        P("dp", None),
        P("sub", "dp"),
        P("sub", "dp"),
        P("dp", "sub"),
    )
    return jax.shard_map(
        shards, mesh=mesh, in_specs=placed, out_specs=P("dp", "sub"), check_vma=False
    )
```

profile of v0, /device:TPU:1, one launch (start us, length us, event | category | flops | bytes accessed | tf_op | source)
XLA Modules:
  0.0 480.4 jit_solution(6949453605712983949)
XLA Ops:
  6.5 0.9 fusion.19
  7.5 9.3 %psum.28 = f32[2]{0:T(128)S(1)} all-reduce(f32[2]{0:T(128)S(1)} %fusion.19), channel_id=1, replica_groups=mesh['dp'=128,'sub'=4] {'sub'}, use_global_device_ids=true, to_apply=%region_1.0 | all-reduce | flops 2 | bytes 16 | tf_op jit(solution)/shard_map/psum | solution.py:46
  16.8 0.8 fusion.30
  17.6 60.3 %all-gather = bf16[128,2,1792]{2,1,0:T(2,128)(2,1)S(1)} all-gather(bf16[1,2,1792]{2,1,0:T(2,128)(2,1)S(1)} %fusion.30), channel_id=1, replica_groups=mesh['dp'=128,'sub'=4] {'dp'}, dimensions={0}, use_global_device_ids=true | all-gather | bytes 924672 | tf_op jit(solution)/shard_map/all_gather | solution.py:48
  78.3 0.5 fusion.7
  78.8 1.5 fusion.6
  80.3 0.7 pad_maximum_fusion.1
  81.0 42.9 %all-reduce.5.cloned.1.call-done = bf16[2,256,144]{1,2,0:T(8,128)(2,1)} async-done(((bf16[2,256,144]{1,2,0:T(8,128)(2,1)}), bf16[2,256,144]{1,2,0:T(8,128)(2,1)}) %all-reduce.5.cloned.1.call-update) | async-done | bytes 147472 | tf_op jit(solution)/shard_map/psum | solution.py:55
  123.9 0.9 convert_element_type.80
  124.9 1.7 fusion.14
  126.8 1.3 dynamic-slice
  128.7 200.7 %all-reduce.9.cloned.1.call-done = f32[256,1792]{1,0:T(8,128)} async-done(((f32[256,1792]{1,0:T(8,128)}), f32[256,1792]{1,0:T(8,128)}) %all-reduce.9.cloned.1.call-update) | async-done | bytes 1835024
  329.4 1.0 fusion.23
  330.4 8.4 %psum.30 = f32[2]{0:T(128)S(1)} all-reduce(f32[2]{0:T(128)S(1)} %get-tuple-element.5), channel_id=1, replica_groups=mesh['dp'=128,'sub'=4] {'sub'}, use_global_device_ids=true, to_apply=%region_8.9 | all-reduce | flops 2 | bytes 16 | tf_op jit(solution)/shard_map/psum | solution.py:65
  339.3 0.9 copy.18
  340.2 40.4 %all_to_all.10 = bf16[128,2,1792]{2,1,0:T(2,128)(2,1)S(1)} all-to-all(bf16[128,2,1792]{2,1,0:T(2,128)(2,1)S(1)} %copy.18), channel_id=1, replica_groups=mesh['dp'=128,'sub'=4] {'dp'}, dimensions={0} | all-to-all | bytes 1835008 | tf_op jit(solution)/shard_map/all_to_all | solution.py:78
  381.0 1.7 fusion.5
  383.1 0.7 pad_maximum_fusion
  383.8 41.9 %all-reduce.7.cloned.1.call-done = bf16[2,256,256]{2,1,0:T(8,128)(2,1)} async-done(((bf16[2,256,256]{2,1,0:T(8,128)(2,1)}), bf16[2,256,256]{2,1,0:T(8,128)(2,1)}) %all-reduce.7.cloned.1.call-update) | async-done | bytes 262160 | tf_op jit(solution)/shard_map/psum | solution.py:80
  425.8 1.0 convert_element_type.88
  427.2 1.3 convert_element_type.95
  428.5 16.4 %all-to-all-start.1 = ((bf16[128,2,1792]{2,1,0:T(2,128)(2,1)}), bf16[128,2,1792]{2,1,0:T(2,128)(2,1)S(1)}, u32[]{:S(2)}, u32[]{:S(2)}) async-start(bf16[128,2,1792]{2,1,0:T(2,128)(2,1)} %convert_element_type.95), calls=%async_computation.1 | async-start | bytes 1835008 | tf_op jit(solution)/shard_map/all_to_all | solution.py:96
  445.9 26.9 %all-to-all-done.1 = bf16[128,2,1792]{2,1,0:T(2,128)(2,1)S(1)} async-done(((bf16[128,2,1792]{2,1,0:T(2,128)(2,1)}), bf16[128,2,1792]{2,1,0:T(2,128)(2,1)S(1)}, u32[]{:S(2)}, u32[]{:S(2)}) %all-to-all-start.1) | async-done | bytes 917536 | tf_op jit(solution)/shard_map/all_to_all | solution.py:96
  472.8 1.1 fusion.3
  (38 shorter events, 2.6 us)
Async XLA Ops:
  6.5 420.2 %copy-start = (bf16[256,1792]{1,0:T(8,128)(2,1)S(1)}, bf16[256,1792]{1,0:T(8,128)(2,1)}, u32[]{:S(2)}) copy-start(bf16[256,1792]{1,0:T(8,128)(2,1)} %param.23) | copy-start | bytes 2752516
  6.5 71.7 %copy-start.2 = (bf16[1792,144]{0,1:T(8,128)(2,1)S(1)}, bf16[1792,144]{0,1:T(8,128)(2,1)}, u32[]{:S(2)}) copy-start(bf16[1792,144]{0,1:T(8,128)(2,1)} %param.16) | copy-start | bytes 1548292
  6.5 117.4 %all-reduce.5.cloned.1.call-start = ((), (), s32[]{:S(2)}) async-start(), calls=%async_computation.2 | async-start | bytes 294912 | tf_op jit(solution)/shard_map/psum | solution.py:55
  78.3 46.6 %copy-start.3 = (bf16[144,1792]{1,0:T(8,128)(2,1)S(1)}, bf16[144,1792]{1,0:T(8,128)(2,1)}, u32[]{:S(2)}) copy-start(bf16[144,1792]{1,0:T(8,128)(2,1)} %param.17) | copy-start | bytes 1548292
  81.0 248.5 %all-reduce.9.cloned.1.call-start = ((), (), s32[]{:S(2)}) async-start(), calls=%async_computation.4 | async-start | bytes 3670016
  124.9 1.8 copy-start.6
  124.9 204.6 %copy-start.4 = (bf16[2,1792]{1,0:T(2,128)(2,1)S(1)}, bf16[2,1792]{1,0:T(2,128)(2,1)}, u32[]{:S(2)}) copy-start(bf16[2,1792]{1,0:T(2,128)(2,1)} %param.12) | copy-start | bytes 21508
  124.9 213.9 %copy-start.5 = (f32[1792]{0:T(1024)S(1)}, f32[1792]{0:T(1024)}, u32[]{:S(2)}) copy-start(f32[1792]{0:T(1024)} %param.18) | copy-start | bytes 21508
  126.6 299.2 %all-reduce.7.cloned.1.call-start = ((), (), s32[]{:S(2)}) async-start(), calls=%async_computation.3 | async-start | bytes 524288 | tf_op jit(solution)/shard_map/psum | solution.py:80
  381.0 1.7 copy-start.1
  427.2 18.4 %copy-start.7 = (f32[2,8]{1,0:T(2,128)S(1)}, f32[2,8]{1,0:T(2,128)}, u32[]{:S(2)}) copy-start(f32[2,8]{1,0:T(2,128)} %param.20) | copy-start | bytes 196
  428.5 44.3 %all-to-all-start.1 = ((bf16[128,2,1792]{2,1,0:T(2,128)(2,1)}), bf16[128,2,1792]{2,1,0:T(2,128)(2,1)S(1)}, u32[]{:S(2)}, u32[]{:S(2)}) async-start(bf16[128,2,1792]{2,1,0:T(2,128)(2,1)} %convert_element_type.95), calls=%async_computation.1 | async-start | bytes 1835008 | tf_op jit(solution)/shard_map/all_to_all | solution.py:96
Sparse Core Ops, SparseCore 0:
  81.1 42.7 all-reduce.4
  127.5 201.8 all-reduce.8
  384.0 41.7 all-reduce.6
where the time goes:
time: 481 us; the launch traced here: 480 us
  waiting for transfers between devices  312 us (65%)
  blocking collectives  118 us (25%)
  starting transfers between devices  16.5 us (3%)
  between operations  14.6 us (3%)
  matrix products  7.9 us (2%)
  other arithmetic  6.25 us (1%)
    unnamed x4, waiting for transfers between devices  201 us
    all_gather x1, blocking collectives, shards(): row_piece = lax.all_gather(dense_normed, 'dp', axis=0, tiled=True)  60.3 us
    psum x1, waiting for transfers between devices, shards(): gate_up = lax.psum(stacked.astype(jnp.bfloat16), 'sub').astype(jnp.float32)  42.9 us
    psum x1, waiting for transfers between devices, shards(): lax.psum(jnp.stack((jnp.dot(flat_rows, expert_gate, preferred_element_typ...  41.9 us
    all_to_all x1, blocking collectives, shards(): lax.all_to_all(outgoing, 'dp', split_axis=0, concat_axis=0, tiled=True)  40.4 us
    all_to_all x1, waiting for transfers between devices, shards(): lax.all_to_all(partial_value.reshape(peer_count, slot_count * expert_span...  26.9 us
    all_to_all x1, starting transfers between devices, shards(): lax.all_to_all(partial_value.reshape(peer_count, slot_count * expert_span...  16.4 us
  transfers between devices with their start and end apart: 4, of which 4 were waited for; matrix products, arithmetic and copies ran while one was open for 0% of the time, Pallas kernels for 0%

commit v1 on v0

v1 whole, which is shorter than its diff:
```python
import functools

import jax
import jax.numpy as jnp
from jax import lax
from jax.experimental import pallas as pl
from jax.experimental.pallas import tpu as pltpu
from jax.sharding import PartitionSpec as P

D = 7168
EH = 2048
EXPERTS = 16
TOP = 8
N = 8
NX = 4
DL = 1792
KC = 256
CHUNKS = DL // KC
HALF = 128
XR = HALF // NX
MESH = pl.DeviceIdType.MESH
F32 = jnp.float32
BF16 = jnp.bfloat16
FAR = (4, 3, 5, 2, 6, 1, 7)
NEAR = (1, 7, 2, 6, 3, 5, 4)


def iota(shape, dim):
    return lax.broadcasted_iota(jnp.int32, shape, dim)


def rounded(value):
    return value.astype(BF16).astype(F32)


def kernel(
    tok,
    newt,
    gain1,
    gate,
    up,
    down,
    gain2,
    ids,
    wts,
    egate,
    eup,
    edown,
    out,
    gv,
    uv,
    w1,
    w2,
    w3,
    w4,
    tb,
    gb,
    ab,
    perm,
    gath,
    xm,
    cw,
    px0,
    px1,
    rx0,
    rx1,
    hid,
    cs,
    cr,
    of,
    s1,
    r1,
    s2,
    r2,
    wsem,
    ag1_s,
    ag1_r,
    ag2_s,
    ag2_r,
    fw_s,
    fw_r,
    rx_s,
    rx_r,
    hx_s,
    hx_r,
    co_s,
    co_r,
    r1_s,
    r1_r,
    r2_s,
    r2_r,
):
    dp = lax.axis_index("dp")
    x = lax.axis_index("sub")
    c = lax.rem(dp, 2)
    y = dp // (2 * N)
    z = lax.rem(dp // 2, N)
    a1 = y * (1 - c) + z * c
    a2 = z * (1 - c) + y * c

    def place(i1, i2):
        return (((i1 * N + i2) * (1 - c) + (i2 * N + i1) * c) * 2 + c, x)

    def peer1(d):
        return place(lax.rem(a1 + d, N), a2)

    def peer2(d):
        return place(a1, lax.rem(a2 + d, N))

    def peerx(d):
        return (dp, lax.rem(x + d, NX))

    sibling = (dp + 1 - 2 * c, x)

    def send(src, dst, ssem, rsem, device):
        return pltpu.make_async_remote_copy(
            src_ref=src,
            dst_ref=dst,
            send_sem=ssem,
            recv_sem=rsem,
            device_id=device,
            device_id_type=MESH,
        )

    barrier = pltpu.get_barrier_semaphore()
    for d in range(1, N):
        pl.semaphore_signal(barrier, inc=1, device_id=peer2(d), device_id_type=MESH)
        pl.semaphore_signal(barrier, inc=1, device_id=peer1(d), device_id_type=MESH)
    for d in range(1, NX):
        pl.semaphore_signal(barrier, inc=1, device_id=peerx(d), device_id_type=MESH)
    pl.semaphore_signal(barrier, inc=1, device_id=sibling, device_id_type=MESH)

    loads = [
        pltpu.make_async_copy(src, dst, wsem.at[i])
        for i, (src, dst) in enumerate(
            (
                (gate, gv),
                (up, uv),
                (gate.at[:, pl.ds(0, 128)], w1.at[pl.ds(0, DL), pl.ds(0, 128)]),
                (up.at[:, pl.ds(0, 128)], w1.at[pl.ds(0, DL), pl.ds(128, 128)]),
                (down, w2.at[pl.ds(0, 144), :]),
                (egate, w3.at[pl.ds(0, DL), pl.ds(0, 256)]),
                (eup, w3.at[pl.ds(0, DL), pl.ds(256, 256)]),
                (edown, w4),
            )
        )
    ]
    for load in loads:
        load.start()

    row = iota((16, KC), 0)
    lane = iota((16, KC), 1)
    odd = lax.rem(row, 2) == 1

    def sums_of_squares(block):
        each = jnp.sum(block * block, axis=1, keepdims=True)
        each = jnp.broadcast_to(each, (16, KC))
        even_sum = jnp.sum(jnp.where(odd, 0.0, each), axis=0, keepdims=True)
        odd_sum = jnp.sum(jnp.where(odd, each, 0.0), axis=0, keepdims=True)
        total = jnp.where(odd, odd_sum, even_sum)
        high = rounded(total)
        middle = rounded(total - high)
        low = total - high - middle
        return jnp.where(
            lane == 32, high, jnp.where(lane == 33, middle, jnp.where(lane == 34, low, 0.0))
        )

    def fill_gain(gain):
        gb[...] = jnp.zeros((16, KC), F32)
        for k in range(CHUNKS):
            gb[2 * k : 2 * k + 2, :] = jnp.broadcast_to(gain[:, KC * k : KC * k + KC], (2, KC))

    stream = tok[...].astype(F32)
    tb[...] = jnp.zeros((16, KC), F32)
    for k in range(CHUNKS):
        tb[2 * k : 2 * k + 2, :] = stream[:, KC * k : KC * k + KC]
    fill_gain(gain1)
    lane2 = iota((2, KC), 1)
    combine = jnp.zeros((2, KC), F32)
    chosen = ids[...]
    weights = wts[...]
    for k in range(TOP):
        combine += jnp.where(chosen[:, k : k + 1] == lax.rem(lane2, EXPERTS), weights[:, k : k + 1], 0.0)
    high = rounded(combine)
    ab[...] = jnp.zeros((16, KC), F32)
    ab[14:16, :] = jnp.where(
        lane2 < EXPERTS, high, jnp.where(lane2 < 2 * EXPERTS, combine - high, 0.0)
    )

    def gather(layer, block, side):
        own_group = c * N + a1
        mine = gath.at[layer, own_group, pl.ds(pl.multiple_of(a2 * 16, 16), 16), :]
        gath[layer, own_group, pl.ds(pl.multiple_of(a2 * 16, 16), 16), :] = jnp.where(
            row < 2 * CHUNKS, block * gb[...], side
        ).astype(BF16)
        if layer == 0:
            pl.semaphore_wait(barrier, 2 * (N - 1) + NX)
        first = [
            send(mine, mine, ag1_s.at[layer, d], ag1_r.at[layer, d], peer2(d)) for d in FAR
        ]
        for copy in first:
            copy.start()
        return first

    def permuted(layer, group):
        moved = jnp.dot(perm[...], gath[layer, group], preferred_element_type=F32).astype(BF16)
        rows = pl.ds(pl.multiple_of(group * 16, 16), 16)
        for k in range(CHUNKS + 1):
            xm[rows, KC * k : KC * k + KC] = moved[16 * k : 16 * k + 16, :]

    def spread(layer, first):
        own_group = c * N + a1
        pending = list(first)
        for copy in first:
            copy.wait_recv()
        line = gath.at[layer, own_group]
        second = {
            d: send(line, line, ag2_s.at[layer, d], ag2_r.at[layer, d], peer1(d)) for d in FAR
        }
        for d in FAR:
            second[d].start()
        pending += second.values()

        def forward(d):
            group = c * N + lax.rem(a1 + N - d, N)
            ref = gath.at[layer, group]
            copy = send(ref, ref, fw_s.at[layer, d], fw_r.at[layer, d], sibling)
            copy.start()
            permuted(layer, group)
            return copy

        forwards = {0: forward(0)}
        for d in NEAR:
            second[d].wait_recv()
            forwards[d] = forward(d)
        pending += forwards.values()
        return pending, forwards

    def rest(layer, forwards):
        for d in (0,) + NEAR:
            forwards[d].wait_recv()
            permuted(layer, (1 - c) * N + lax.rem(a2 + N - d, N))

    halves = (c, 1 - c)

    def half_rows(h):
        return pl.ds(pl.multiple_of(halves[h] * HALF, HALF), HALF)

    def part_rows(h, index):
        return pl.ds(pl.multiple_of(halves[h] * HALF + index * XR, XR), XR)

    def project(layer, h, px, rx, weight):
        px[half_rows(h), :] = jnp.dot(
            xm[half_rows(h), :], weight[...], preferred_element_type=F32
        ).astype(BF16)
        copies = [
            send(
                px.at[part_rows(h, lax.rem(x + d, NX)), :],
                rx.at[h, d],
                rx_s.at[layer, h, d],
                rx_r.at[layer, h, d],
                peerx(d),
            )
            for d in (2, 1, 3)
        ]
        for copy in copies:
            copy.start()
        return copies

    def activate(layer, h, px, rx, copies):
        total = px[part_rows(h, x), :].astype(F32)
        for copy, d in zip(copies, (2, 1, 3)):
            copy.wait_recv()
            total = total + rx[h, d].astype(F32)
        tail = total[:, total.shape[1] - 128 :]
        spot = iota((XR, 128), 1)
        if layer == 0:
            used = (spot >= 96) & (spot < 99)
        else:
            used = spot < 3
        squares = jnp.sum(jnp.where(used, tail, 0.0), axis=1, keepdims=True)
        scale = lax.rsqrt(squares / D + 1e-06)
        if layer == 0:
            main = jax.nn.silu(total[:, :128] * scale) * (total[:, 128:256] * scale)
            last = jax.nn.silu(tail * scale) * (pltpu.roll(tail, 64, 1) * scale)
            last = jnp.where(spot < 16, last, 0.0)
            value = jnp.concatenate((main, last), axis=1)
        else:
            value = jax.nn.silu(total[:, :256] * scale) * (total[:, 256:512] * scale)
            share = cw[part_rows(h, x), :]
            value = value * jnp.concatenate((share, share), axis=1)
        rows = part_rows(h, x)
        hid[layer, rows, :] = value.astype(BF16)
        mine = hid.at[layer, rows, :]
        out_copies = [
            send(mine, mine, hx_s.at[layer, h, d], hx_r.at[layer, h, d], peerx(d)) for d in (2, 1, 3)
        ]
        for copy in out_copies:
            copy.start()
        return out_copies

    def lower(layer, weight, hx):
        for copy in hx[0]:
            copy.wait_recv()
        value = hid[layer, half_rows(0), :]
        for k in range(CHUNKS):
            of[:, KC * k : KC * k + KC] = jnp.dot(
                value, weight[:, KC * k : KC * k + KC], preferred_element_type=F32
            )
        for copy in hx[1]:
            copy.wait_recv()
        value = hid[layer, half_rows(1), :]
        for k in range(CHUNKS):
            cs[layer, :, KC * k : KC * k + KC] = jnp.dot(
                value, weight[:, KC * k : KC * k + KC], preferred_element_type=F32
            ).astype(BF16)

    def chunk_rows(index):
        return pl.ds(pl.multiple_of(index * 16, 16), 16)

    def scatter(layer):
        cross = {}
        for d in FAR + (0,):
            rows = chunk_rows(lax.rem(a2 + d, N))
            cross[d] = send(
                cs.at[layer, rows, :],
                cr.at[layer, rows, :],
                co_s.at[layer, d],
                co_r.at[layer, d],
                sibling,
            )
            cross[d].start()
        pending = list(cross.values())
        first = {}
        for d in FAR + (0,):
            rows = chunk_rows(lax.rem(a1 + d, N))
            cross[d].wait_recv()
            value = of[rows, :] + cr[layer, rows, :].astype(F32)
            if d:
                s1[layer, rows, :] = value.astype(BF16)
                first[d] = send(
                    s1.at[layer, rows, :],
                    r1.at[layer, d],
                    r1_s.at[layer, d],
                    r1_r.at[layer, d],
                    peer1(d),
                )
                first[d].start()
        total = value
        for d in NEAR:
            first[d].wait_recv()
            total = total + r1[layer, d].astype(F32)
        pending += first.values()
        total = total.astype(BF16)
        stacked = jnp.concatenate(
            [total[:, KC * k : KC * k + KC] for k in range(CHUNKS)] + [jnp.zeros((16, KC), BF16)],
            axis=0,
        )
        s2[layer] = jnp.dot(perm[...], stacked, preferred_element_type=F32).astype(BF16)
        second = {}
        for d in FAR:
            second[d] = send(
                s2.at[layer, chunk_rows(lax.rem(a2 + d, N)), :],
                r2.at[layer, d],
                r2_s.at[layer, d],
                r2_r.at[layer, d],
                peer2(d),
            )
            second[d].start()
        total = s2[layer, chunk_rows(a2), :].astype(F32)
        for d in NEAR:
            second[d].wait_recv()
            total = total + r2[layer, d].astype(F32)
        pending += second.values()
        return total, pending

    def layer_of(layer, block, side, px, rx, w_in, w_out, prepare, loads_in, loads_out):
        first = gather(layer, block, side)
        prepare()
        pending, forwards = spread(layer, first)
        for load in loads_in:
            load.wait()
        if layer == 0:
            cw[half_rows(0), :] = jnp.dot(
                xm[half_rows(0), DL:], selector, preferred_element_type=F32
            )
        x0 = project(layer, 0, px, rx, w_in)
        rest(layer, forwards)
        x1 = project(layer, 1, px, rx, w_in)
        if layer == 0:
            cw[half_rows(1), :] = jnp.dot(
                xm[half_rows(1), DL:], selector, preferred_element_type=F32
            )
        h0 = activate(layer, 0, px, rx, x0)
        h1 = activate(layer, 1, px, rx, x1)
        for load in loads_out:
            load.wait()
        lower(layer, w_out, (h0, h1))
        total, more = scatter(layer)
        return total, pending + x0 + x1 + h0 + h1 + more

    expert = dp // (EH // 256)
    at = iota((KC, 128), 0)
    selector = ((at == expert) | (at == expert + EXPERTS)).astype(F32).astype(BF16)

    def prepare():
        to = iota((128, 128), 0)
        source = lax.rem(to // 2, 8) * 16 + (to // 16) * 2 + lax.rem(to, 2)
        perm[...] = (source == iota((128, 128), 1)).astype(F32).astype(BF16)
        side_row = iota((KC, 128), 0)
        side_lane = iota((KC, 128), 1)
        is_part = (side_row >= 32) & (side_row < 35)
        w1[DL:, :256] = jnp.zeros((KC, 256), BF16)
        w1[DL:, 256:] = (is_part & (side_lane == side_row + 64)).astype(F32).astype(BF16)
        w2[144:, :] = jnp.zeros((112, DL), BF16)
        w3[DL:, :512] = jnp.zeros((KC, 512), BF16)
        w3[:DL, 512:] = jnp.zeros((DL, 128), BF16)
        w3[DL:, 512:] = (is_part & (side_lane == side_row - 32)).astype(F32).astype(BF16)
        loads[0].wait()
        loads[1].wait()

        def tails(i, carry):
            rows = pl.ds(pl.multiple_of(i * KC, KC), KC)
            blank = jnp.zeros((KC, 48), BF16)
            w1[rows, 256:] = jnp.concatenate((gv[rows, 128:], blank, uv[rows, 128:], blank), axis=1)
            return carry

        lax.fori_loop(0, CHUNKS, tails, 0)

    tokens_block = tb[...]
    side = jnp.where(row >= 14, ab[...] + sums_of_squares(tokens_block), 0.0)
    dense, pending = layer_of(
        0, tokens_block, side, px0, rx0, w1, w2, prepare, loads[2:4], loads[4:5]
    )
    fill_gain(gain2)
    mixed = rounded(tb[...] + dense)
    mixed = jnp.where(row < 2 * CHUNKS, mixed, 0.0)
    tb[...] = mixed
    side = jnp.where(row >= 14, sums_of_squares(mixed), 0.0)
    routed, more = layer_of(
        1, mixed, side, px1, rx1, w3, w4, lambda: None, loads[5:7], loads[7:]
    )
    tb[...] = tb[...] + routed
    live = iota((2, KC), 0) < newt[0]
    for k in range(CHUNKS):
        out[:, KC * k : KC * k + KC] = jnp.where(live, tb[2 * k : 2 * k + 2, :], 0.0)
    for copy in pending + more:
        copy.wait_send()


def shards(
    tokens,
    new_tokens,
    dense_gain,
    dense_gate,
    dense_up,
    dense_down,
    moe_gain,
    expert_ids,
    expert_weights,
    expert_gate,
    expert_up,
    expert_down,
):
    vmem = pl.BlockSpec(memory_space=pltpu.VMEM)
    smem = pl.BlockSpec(memory_space=pltpu.SMEM)
    anywhere = pl.BlockSpec(memory_space=pl.ANY)
    sems = pltpu.SemaphoreType.DMA
    result = pl.pallas_call(
        kernel,
        out_shape=jax.ShapeDtypeStruct((2, DL), F32),
        in_specs=[
            vmem,
            smem,
            vmem,
            anywhere,
            anywhere,
            anywhere,
            vmem,
            vmem,
            vmem,
            anywhere,
            anywhere,
            anywhere,
        ],
        out_specs=vmem,
        scratch_shapes=[
            pltpu.VMEM((DL, 144), BF16),
            pltpu.VMEM((DL, 144), BF16),
            pltpu.VMEM((DL + KC, 384), BF16),
            pltpu.VMEM((256, DL), BF16),
            pltpu.VMEM((DL + KC, 640), BF16),
            pltpu.VMEM((256, DL), BF16),
            pltpu.VMEM((16, KC), F32),
            pltpu.VMEM((16, KC), F32),
            pltpu.VMEM((16, KC), F32),
            pltpu.VMEM((128, 128), BF16),
            pltpu.VMEM((2, 2 * N, 128, KC), BF16),
            pltpu.VMEM((2 * HALF, DL + KC), BF16),
            pltpu.VMEM((2 * HALF, 128), F32),
            pltpu.VMEM((2 * HALF, 384), BF16),
            pltpu.VMEM((2 * HALF, 640), BF16),
            pltpu.VMEM((2, NX, XR, 384), BF16),
            pltpu.VMEM((2, NX, XR, 640), BF16),
            pltpu.VMEM((2, 2 * HALF, 256), BF16),
            pltpu.VMEM((2, HALF, DL), BF16),
            pltpu.VMEM((2, HALF, DL), BF16),
            pltpu.VMEM((HALF, DL), F32),
            pltpu.VMEM((2, HALF, DL), BF16),
            pltpu.VMEM((2, N, 16, DL), BF16),
            pltpu.VMEM((2, 128, KC), BF16),
            pltpu.VMEM((2, N, 16, KC), BF16),
            sems((8,)),
            sems((2, N)),
            sems((2, N)),
            sems((2, N)),
            sems((2, N)),
            sems((2, N)),
            sems((2, N)),
            sems((2, 2, NX)),
            sems((2, 2, NX)),
            sems((2, 2, NX)),
            sems((2, 2, NX)),
            sems((2, N)),
            sems((2, N)),
            sems((2, N)),
            sems((2, N)),
            sems((2, N)),
            sems((2, N)),
        ],
        compiler_params=pltpu.CompilerParams(
            collective_id=0, has_side_effects=True, vmem_limit_bytes=48 * 1024 * 1024
        ),
        name="layers",
    )(
        tokens,
        new_tokens,
        dense_gain.reshape(1, DL),
        dense_gate,
        dense_up,
        dense_down,
        moe_gain.reshape(1, DL),
        expert_ids,
        expert_weights,
        expert_gate,
        expert_up,
        expert_down,
    )
    return result.astype(BF16)


def solution(mesh):
    placed = (
        P("dp", "sub"),
        P("dp"),
        P("sub"),
        P("sub", "dp"),
        P("sub", "dp"),
        P("dp", "sub"),
        P("sub"),
        P("dp", None),
        P("dp", None),
        P("sub", "dp"),
        P("sub", "dp"),
        P("dp", "sub"),
    )
    return jax.shard_map(
        shards, mesh=mesh, in_specs=placed, out_specs=P("dp", "sub"), check_vma=False
    )
```

time: 481 us -> 100 us (0.21)
  waiting for transfers between devices: 312 us -> 0 us
  blocking collectives: 118 us -> 0 us
  Pallas kernels: 0 us -> 92.8 us
  starting transfers between devices: 16.5 us -> 0 us
  between operations: 14.6 us -> 0.78 us
  matrix products: 7.9 us -> 0 us
  other arithmetic: 6.25 us -> 0.6 us
    unnamed x4 -> x0, waiting for transfers between devices: 201 us -> none
    pallas_call x0 -> x1, Pallas kernels: none -> 92.8 us  [shards(): pl.pallas_call(kernel, out_shape=jax.ShapeDtypeStruct((2, DL), F32), in_s...]
    psum x2 -> x0, waiting for transfers between devices: 84.8 us -> none  [the longest x1 42.9 us: shards(): gate_up = lax.psum(stacked.astype(jnp.bfloat16), 'sub').astype(jnp.float32)]
    all_gather x1 -> x0, blocking collectives: 60.3 us -> none  [shards(): row_piece = lax.all_gather(dense_normed, 'dp', axis=0, tiled=True)]
    all_to_all x1 -> x0, blocking collectives: 40.4 us -> none  [shards(): lax.all_to_all(outgoing, 'dp', split_axis=0, concat_axis=0, tiled=True)]
    all_to_all x1 -> x0, waiting for transfers between devices: 26.9 us -> none  [shards(): lax.all_to_all(partial_value.reshape(peer_count, slot_count * expert_span...]
    psum x2 -> x0, blocking collectives: 17.7 us -> none  [the longest x1 9.3 us: shards(): totals = lax.psum(jnp.sum(token_stream * token_stream, axis=1), 'sub')]
    all_to_all x1 -> x0, starting transfers between devices: 16.4 us -> none  [shards(): lax.all_to_all(partial_value.reshape(peer_count, slot_count * expert_span...]
  transfers between devices with their start and end apart: 4 -> 0, of which waited for: 4 -> 0; matrix products, arithmetic and copies ran while one was open for 0% -> 0% of each run, Pallas kernels for 0% -> 0%
where the time goes in v1:
time: 100 us
  Pallas kernels  92.8 us (93%)
  local copies, waits for them, and re-layouts  5.9 us (6%)
    pallas_call x1, Pallas kernels, shards(): pl.pallas_call(kernel, out_shape=jax.ShapeDtypeStruct((2, DL), F32), in_s...  92.8 us
    unnamed x18, local copies, waits for them, and re-layouts  5.19 us

profile of v1, /device:TPU:1, one launch (start us, length us, event | category | flops | bytes accessed | tf_op | source)
XLA Modules:
  0.0 100.1 jit_solution(2028879988396804237)
XLA Ops:
  0.0 0.0 copy-start.7
  0.7 0.7 reshape.6.gain1
  1.4 0.0 copy-done.7
  1.4 0.0 copy-start.4
  1.4 0.0 copy-start.5
  1.4 0.0 copy-start.6
  1.4 1.4 %copy.13.gate = bf16[1792,144]{1,0:T(8,128)(2,1)S(1)} copy(bf16[1792,144]{0,1:T(8,128)(2,1)} %param.15) | data formatting | bytes 1032192 | tf_op args[3]
  2.8 0.0 copy-start
  2.8 0.0 copy-start.3
  2.8 1.5 %copy.14.up = bf16[1792,144]{1,0:T(8,128)(2,1)S(1)} copy(bf16[1792,144]{0,1:T(8,128)(2,1)} %param.16) | data formatting | bytes 1032192 | tf_op args[4]
  4.3 0.0 copy-done.4
  4.3 0.0 copy-done.5
  4.3 0.0 copy-done.6
  4.3 0.0 copy-done
  4.3 0.0 copy-done.3
  4.3 0.0 copy-start.1
  4.3 1.2 %copy-done.1 = bf16[1792,256]{1,0:T(8,128)(2,1)S(1)} copy-done((bf16[1792,256]{1,0:T(8,128)(2,1)S(1)}, bf16[1792,256]{1,0:T(8,128)(2,1)}, u32[]{:S(2)}) %copy-start.1) | copy-done | bytes 917528
  5.5 0.0 copy-start.2
  5.5 1.2 %copy-done.2 = bf16[256,1792]{1,0:T(8,128)(2,1)S(1)} copy-done((bf16[256,1792]{1,0:T(8,128)(2,1)S(1)}, bf16[256,1792]{1,0:T(8,128)(2,1)}, u32[]{:S(2)}) %copy-start.2) | copy-done | bytes 917528
  6.7 92.8 %layers.1 = f32[2,1792]{1,0:T(2,128)S(1)} custom-call(bf16[2,1792]{1,0:T(2,128)(2,1)S(1)} %copy-done.4, s32[1]{0:T(128)S(6)} %copy.15.newt, f32[1,1792]{1,0:T(1,128)S(1)} %reshape.6.gain1, bf16[1792,144]{1,0:T(8,128)(2,1)S(1)} %copy.13.gate, bf16[1792,144]{1,0:T(8,128)(2,1)S(1)} %copy.14.up, bf16[144,1792]{1,0:T(8,128)(2,1)S(1)} %copy-done.3, ...), custom_call_target="tpu_custom_call" | custom-call | tf_op jit(solution)/shard_map/layers/pallas_call | solution.py:469
  99.5 0.6 convert_element_type.3
  (1 shorter events, 0.0 us)
Async XLA Ops:
  0.0 1.4 %copy-start.7 = (f32[1792]{0:T(1024)S(1)}, f32[1792]{0:T(1024)}, u32[]{:S(2)}) copy-start(f32[1792]{0:T(1024)} %param.18) | copy-start | bytes 21508
  1.4 2.9 %copy-start.4 = (bf16[2,1792]{1,0:T(2,128)(2,1)S(1)}, bf16[2,1792]{1,0:T(2,128)(2,1)}, u32[]{:S(2)}) copy-start(bf16[2,1792]{1,0:T(2,128)(2,1)} %tok.1) | copy-start | bytes 21508
  1.4 2.9 %copy-start.5 = (s32[2,8]{1,0:T(2,128)S(1)}, s32[2,8]{1,0:T(2,128)}, u32[]{:S(2)}) copy-start(s32[2,8]{1,0:T(2,128)} %ids.1) | copy-start | bytes 196
  1.4 2.9 %copy-start.6 = (f32[2,8]{1,0:T(2,128)S(1)}, f32[2,8]{1,0:T(2,128)}, u32[]{:S(2)}) copy-start(f32[2,8]{1,0:T(2,128)} %wts.1) | copy-start | bytes 196
  2.8 1.5 %copy-start = (bf16[1792,256]{1,0:T(8,128)(2,1)S(1)}, bf16[1792,256]{1,0:T(8,128)(2,1)}, u32[]{:S(2)}) copy-start(bf16[1792,256]{1,0:T(8,128)(2,1)} %egate.1) | copy-start | bytes 2752516
  2.8 1.5 %copy-start.3 = (bf16[144,1792]{1,0:T(8,128)(2,1)S(1)}, bf16[144,1792]{1,0:T(8,128)(2,1)}, u32[]{:S(2)}) copy-start(bf16[144,1792]{1,0:T(8,128)(2,1)} %down.1) | copy-start | bytes 1548292
  4.3 1.2 %copy-start.1 = (bf16[1792,256]{1,0:T(8,128)(2,1)S(1)}, bf16[1792,256]{1,0:T(8,128)(2,1)}, u32[]{:S(2)}) copy-start(bf16[1792,256]{1,0:T(8,128)(2,1)} %eup.1) | copy-start | bytes 2752516
  5.5 1.2 %copy-start.2 = (bf16[256,1792]{1,0:T(8,128)(2,1)S(1)}, bf16[256,1792]{1,0:T(8,128)(2,1)}, u32[]{:S(2)}) copy-start(bf16[256,1792]{1,0:T(8,128)(2,1)} %edown.1) | copy-start | bytes 2752516

commit v2 on v1

--- a/solution.py
+++ b/solution.py
@@ -47,8 +47,6 @@
     eup,
     edown,
     out,
-    gv,
-    uv,
     w1,
     w2,
     w3,
@@ -134,10 +132,10 @@
         pltpu.make_async_copy(src, dst, wsem.at[i])
         for i, (src, dst) in enumerate(
             (
-                (gate, gv),
-                (up, uv),
-                (gate.at[:, pl.ds(0, 128)], w1.at[pl.ds(0, DL), pl.ds(0, 128)]),
-                (up.at[:, pl.ds(0, 128)], w1.at[pl.ds(0, DL), pl.ds(128, 128)]),
+                (gate.at[pl.ds(0, 128), :], w1.at[pl.ds(0, 128), pl.ds(0, DL)]),
+                (up.at[pl.ds(0, 128), :], w1.at[pl.ds(128, 128), pl.ds(0, DL)]),
+                (gate.at[pl.ds(128, 16), :], w1.at[pl.ds(256, 16), pl.ds(0, DL)]),
+                (up.at[pl.ds(128, 16), :], w1.at[pl.ds(320, 16), pl.ds(0, DL)]),
                 (down, w2.at[pl.ds(0, 144), :]),
                 (egate, w3.at[pl.ds(0, DL), pl.ds(0, 256)]),
                 (eup, w3.at[pl.ds(0, DL), pl.ds(256, 256)]),
@@ -168,7 +166,7 @@
     def fill_gain(gain):
         gb[...] = jnp.zeros((16, KC), F32)
         for k in range(CHUNKS):
-            gb[2 * k : 2 * k + 2, :] = jnp.broadcast_to(gain[:, KC * k : KC * k + KC], (2, KC))
+            gb[2 * k : 2 * k + 2, :] = jnp.broadcast_to(gain[KC * k : KC * k + KC][None, :], (2, KC))
 
     stream = tok[...].astype(F32)
     tb[...] = jnp.zeros((16, KC), F32)
@@ -250,8 +248,11 @@
         return pl.ds(pl.multiple_of(halves[h] * HALF + index * XR, XR), XR)
 
     def project(layer, h, px, rx, weight):
-        px[half_rows(h), :] = jnp.dot(
-            xm[half_rows(h), :], weight[...], preferred_element_type=F32
+        px[half_rows(h), :] = lax.dot_general(
+            xm[half_rows(h), :],
+            weight[...],
+            (((1,), (1 - layer,)), ((), ())),
+            preferred_element_type=F32,
         ).astype(BF16)
         copies = [
             send(
@@ -410,27 +411,22 @@
         side_row = iota((KC, 128), 0)
         side_lane = iota((KC, 128), 1)
         is_part = (side_row >= 32) & (side_row < 35)
-        w1[DL:, :256] = jnp.zeros((KC, 256), BF16)
-        w1[DL:, 256:] = (is_part & (side_lane == side_row + 64)).astype(F32).astype(BF16)
+        w1[:256, DL:] = jnp.zeros((256, KC), BF16)
+        w1[272:320, :DL] = jnp.zeros((48, DL), BF16)
+        w1[336:, :DL] = jnp.zeros((48, DL), BF16)
+        to_row = iota((128, KC), 0)
+        to_lane = iota((128, KC), 1)
+        wanted = (to_lane >= 32) & (to_lane < 35) & (to_row == to_lane + 64)
+        w1[256:, DL:] = wanted.astype(F32).astype(BF16)
         w2[144:, :] = jnp.zeros((112, DL), BF16)
         w3[DL:, :512] = jnp.zeros((KC, 512), BF16)
         w3[:DL, 512:] = jnp.zeros((DL, 128), BF16)
         w3[DL:, 512:] = (is_part & (side_lane == side_row - 32)).astype(F32).astype(BF16)
-        loads[0].wait()
-        loads[1].wait()
-
-        def tails(i, carry):
-            rows = pl.ds(pl.multiple_of(i * KC, KC), KC)
-            blank = jnp.zeros((KC, 48), BF16)
-            w1[rows, 256:] = jnp.concatenate((gv[rows, 128:], blank, uv[rows, 128:], blank), axis=1)
-            return carry
-
-        lax.fori_loop(0, CHUNKS, tails, 0)
 
     tokens_block = tb[...]
     side = jnp.where(row >= 14, ab[...] + sums_of_squares(tokens_block), 0.0)
     dense, pending = layer_of(
-        0, tokens_block, side, px0, rx0, w1, w2, prepare, loads[2:4], loads[4:5]
+        0, tokens_block, side, px0, rx0, w1, w2, prepare, loads[0:4], loads[4:5]
     )
     fill_gain(gain2)
     mixed = rounded(tb[...] + dense)
@@ -464,7 +460,7 @@
 ):
     vmem = pl.BlockSpec(memory_space=pltpu.VMEM)
     smem = pl.BlockSpec(memory_space=pltpu.SMEM)
-    anywhere = pl.BlockSpec(memory_space=pl.ANY)
+    anywhere = pl.BlockSpec(memory_space=pltpu.HBM)
     sems = pltpu.SemaphoreType.DMA
     result = pl.pallas_call(
         kernel,
@@ -485,9 +481,7 @@
         ],
         out_specs=vmem,
         scratch_shapes=[
-            pltpu.VMEM((DL, 144), BF16),
-            pltpu.VMEM((DL, 144), BF16),
-            pltpu.VMEM((DL + KC, 384), BF16),
+            pltpu.VMEM((384, DL + KC), BF16),
             pltpu.VMEM((256, DL), BF16),
             pltpu.VMEM((DL + KC, 640), BF16),
             pltpu.VMEM((256, DL), BF16),
@@ -529,17 +523,17 @@
             sems((2, N)),
         ],
         compiler_params=pltpu.CompilerParams(
-            collective_id=0, has_side_effects=True, vmem_limit_bytes=48 * 1024 * 1024
+            collective_id=0, has_side_effects=True, vmem_limit_bytes=60 * 1024 * 1024
         ),
         name="layers",
     )(
         tokens,
         new_tokens,
-        dense_gain.reshape(1, DL),
-        dense_gate,
-        dense_up,
+        dense_gain,
+        dense_gate.T,
+        dense_up.T,
         dense_down,
-        moe_gain.reshape(1, DL),
+        moe_gain,
         expert_ids,
         expert_weights,
         expert_gate,

time: 100 us -> 96.7 us (0.967)
  local copies, waits for them, and re-layouts: 5.9 us -> 0 us
  Pallas kernels: 92.8 us -> 94.5 us
    unnamed x18 -> x0, local copies, waits for them, and re-layouts: 5.19 us -> none
    pallas_call x1, Pallas kernels: 92.8 us -> 94.5 us  [shards(): pl.pallas_call(kernel, out_shape=jax.ShapeDtypeStruct((2, DL), F32), in_s...]
where the time goes in v2:
time: 96.7 us; the launch traced here: 96.5 us
  Pallas kernels  94.5 us (98%)
  other arithmetic  1.31 us (1%)
    pallas_call x1, Pallas kernels, shards(): pl.pallas_call(kernel, out_shape=jax.ShapeDtypeStruct((2, DL), F32), in_s...  94.5 us

profile of v2, /device:TPU:1, one launch (start us, length us, event | category | flops | bytes accessed | tf_op | source)
XLA Modules:
  0.0 96.5 jit_solution(5823623905711137653)
XLA Ops:
  0.7 94.5 %layers.1 = f32[2,1792]{1,0:T(2,128)} custom-call(bf16[2,1792]{1,0:T(2,128)(2,1)} %tok.1, s32[1]{0:T(128)S(6)} %copy.13.newt, f32[1792]{0:T(1024)} %gain1.1, bf16[144,1792]{1,0:T(8,128)(2,1)} %bitcast.2, bf16[144,1792]{1,0:T(8,128)(2,1)} %bitcast.3, bf16[144,1792]{1,0:T(8,128)(2,1)} %down.1, f32[1792]{0:T(1024)} %gain2.1, s32[2,8]{1,0:T(2,128)} %ids.1, ...), custom_call_target="tpu_custom_call" | custom-call | tf_op jit(solution)/shard_map/layers/pallas_call | solution.py:465
  95.2 1.3 %convert_element_type.3 = bf16[2,1792]{1,0:T(2,128)(2,1)} convert(f32[2,1792]{1,0:T(2,128)} %layers.1) | non-fusion elementwise | flops 3584 | bytes 21504 | tf_op jit(solution)/shard_map/convert_element_type | solution.py:543

commit v3 on v2

--- a/solution.py
+++ b/solution.py
@@ -23,6 +23,7 @@
 BF16 = jnp.bfloat16
 FAR = (4, 3, 5, 2, 6, 1, 7)
 NEAR = (1, 7, 2, 6, 3, 5, 4)
+BATCHES = ((3, 5, 4, 0), (1, 7, 2, 6))
 
 
 def iota(shape, dim):
@@ -186,9 +187,9 @@
     )
 
     def gather(layer, block, side):
-        own_group = c * N + a1
-        mine = gath.at[layer, own_group, pl.ds(pl.multiple_of(a2 * 16, 16), 16), :]
-        gath[layer, own_group, pl.ds(pl.multiple_of(a2 * 16, 16), 16), :] = jnp.where(
+        place_rows = chunk_rows(a2)
+        mine = gath.at[layer, 0, place_rows, :]
+        gath[layer, 0, place_rows, :] = jnp.where(
             row < 2 * CHUNKS, block * gb[...], side
         ).astype(BF16)
         if layer == 0:
@@ -198,81 +199,84 @@
         ]
         for copy in first:
             copy.start()
-        return first
-
-    def permuted(layer, group):
-        moved = jnp.dot(perm[...], gath[layer, group], preferred_element_type=F32).astype(BF16)
-        rows = pl.ds(pl.multiple_of(group * 16, 16), 16)
-        for k in range(CHUNKS + 1):
-            xm[rows, KC * k : KC * k + KC] = moved[16 * k : 16 * k + 16, :]
-
-    def spread(layer, first):
-        own_group = c * N + a1
-        pending = list(first)
         for copy in first:
             copy.wait_recv()
-        line = gath.at[layer, own_group]
-        second = {
-            d: send(line, line, ag2_s.at[layer, d], ag2_r.at[layer, d], peer1(d)) for d in FAR
-        }
+        line = gath.at[layer, 0]
+        second = {}
         for d in FAR:
+            second[d] = send(
+                line, gath.at[layer, d], ag2_s.at[layer, d], ag2_r.at[layer, d], peer1(d)
+            )
             second[d].start()
-        pending += second.values()
-
-        def forward(d):
-            group = c * N + lax.rem(a1 + N - d, N)
-            ref = gath.at[layer, group]
-            copy = send(ref, ref, fw_s.at[layer, d], fw_r.at[layer, d], sibling)
-            copy.start()
-            permuted(layer, group)
-            return copy
-
-        forwards = {0: forward(0)}
-        for d in NEAR:
-            second[d].wait_recv()
-            forwards[d] = forward(d)
-        pending += forwards.values()
-        return pending, forwards
-
-    def rest(layer, forwards):
-        for d in (0,) + NEAR:
+        forwards = {0: forward(layer, 0)}
+        return first, second, forwards
+
+    def forward(layer, d):
+        copy = send(
+            gath.at[layer, d],
+            gath.at[layer, N + d],
+            fw_s.at[layer, d],
+            fw_r.at[layer, d],
+            sibling,
+        )
+        copy.start()
+        return copy
+
+    def permuted(layer, batch, other):
+        groups = [gath[layer, N * other + d] for d in BATCHES[batch]]
+        moved = jnp.dot(
+            perm[...], jnp.concatenate(groups, axis=1), preferred_element_type=F32
+        ).astype(BF16)
+        for q in range(len(groups)):
+            start = HALF * batch + 64 * other + 16 * q
+            for k in range(CHUNKS + 1):
+                xm[start : start + 16, KC * k : KC * k + KC] = moved[
+                    16 * k : 16 * k + 16, KC * q : KC * q + KC
+                ]
+
+    def receive(layer, batch, second, forwards):
+        for d in BATCHES[batch]:
+            if d:
+                second[d].wait_recv()
+                forwards[d] = forward(layer, d)
+        permuted(layer, batch, 0)
+        for d in BATCHES[batch]:
             forwards[d].wait_recv()
-            permuted(layer, (1 - c) * N + lax.rem(a2 + N - d, N))
-
-    halves = (c, 1 - c)
-
-    def half_rows(h):
-        return pl.ds(pl.multiple_of(halves[h] * HALF, HALF), HALF)
-
-    def part_rows(h, index):
-        return pl.ds(pl.multiple_of(halves[h] * HALF + index * XR, XR), XR)
-
-    def project(layer, h, px, rx, weight):
-        px[half_rows(h), :] = lax.dot_general(
-            xm[half_rows(h), :],
+        permuted(layer, batch, 1)
+
+    def part_rows(batch, index):
+        return pl.ds(pl.multiple_of(batch * HALF + index * XR, XR), XR)
+
+    def project(layer, batch, px, rx, weight):
+        rows = pl.ds(batch * HALF, HALF)
+        px[rows, :] = lax.dot_general(
+            xm[rows, :],
             weight[...],
             (((1,), (1 - layer,)), ((), ())),
             preferred_element_type=F32,
         ).astype(BF16)
         copies = [
             send(
-                px.at[part_rows(h, lax.rem(x + d, NX)), :],
-                rx.at[h, d],
-                rx_s.at[layer, h, d],
-                rx_r.at[layer, h, d],
+                px.at[part_rows(batch, lax.rem(x + d, NX)), :],
+                rx.at[batch, d],
+                rx_s.at[layer, batch, d],
+                rx_r.at[layer, batch, d],
                 peerx(d),
             )
             for d in (2, 1, 3)
         ]
         for copy in copies:
             copy.start()
+        if layer == 0:
+            cw[rows, :] = jnp.dot(xm[rows, DL:], selector, preferred_element_type=F32)
         return copies
 
-    def activate(layer, h, px, rx, copies):
-        total = px[part_rows(h, x), :].astype(F32)
+    def activate(layer, batch, px, rx, copies):
+        rows = part_rows(batch, x)
+        total = px[rows, :].astype(F32)
         for copy, d in zip(copies, (2, 1, 3)):
             copy.wait_recv()
-            total = total + rx[h, d].astype(F32)
+            total = total + rx[batch, d].astype(F32)
         tail = total[:, total.shape[1] - 128 :]
         spot = iota((XR, 128), 1)
         if layer == 0:
@@ -288,70 +292,76 @@
             value = jnp.concatenate((main, last), axis=1)
         else:
             value = jax.nn.silu(total[:, :256] * scale) * (total[:, 256:512] * scale)
-            share = cw[part_rows(h, x), :]
+            share = cw[rows, :]
             value = value * jnp.concatenate((share, share), axis=1)
-        rows = part_rows(h, x)
         hid[layer, rows, :] = value.astype(BF16)
         mine = hid.at[layer, rows, :]
         out_copies = [
-            send(mine, mine, hx_s.at[layer, h, d], hx_r.at[layer, h, d], peerx(d)) for d in (2, 1, 3)
+            send(
+                mine,
+                mine,
+                hx_s.at[layer, batch, d],
+                hx_r.at[layer, batch, d],
+                peerx(d),
+            )
+            for d in (2, 1, 3)
         ]
         for copy in out_copies:
             copy.start()
         return out_copies
 
-    def lower(layer, weight, hx):
-        for copy in hx[0]:
+    def lower(layer, batch, weight, copies):
+        for copy in copies:
             copy.wait_recv()
-        value = hid[layer, half_rows(0), :]
+        value = hid[layer, HALF * batch : HALF * batch + HALF, :]
+        rows = pl.ds(64 * batch, 64)
         for k in range(CHUNKS):
-            of[:, KC * k : KC * k + KC] = jnp.dot(
-                value, weight[:, KC * k : KC * k + KC], preferred_element_type=F32
+            part = jnp.dot(value, weight[:, KC * k : KC * k + KC], preferred_element_type=F32)
+            of[rows, KC * k : KC * k + KC] = part[:64, :]
+            cs[layer, rows, KC * k : KC * k + KC] = part[64:, :].astype(BF16)
+        cross = []
+        for q, d in enumerate(BATCHES[batch]):
+            part_of = pl.ds(64 * batch + 16 * q, 16)
+            cross.append(
+                send(
+                    cs.at[layer, part_of, :],
+                    cr.at[layer, part_of, :],
+                    co_s.at[layer, d],
+                    co_r.at[layer, d],
+                    sibling,
+                )
             )
-        for copy in hx[1]:
-            copy.wait_recv()
-        value = hid[layer, half_rows(1), :]
-        for k in range(CHUNKS):
-            cs[layer, :, KC * k : KC * k + KC] = jnp.dot(
-                value, weight[:, KC * k : KC * k + KC], preferred_element_type=F32
-            ).astype(BF16)
+            cross[q].start()
+        return cross
 
     def chunk_rows(index):
         return pl.ds(pl.multiple_of(index * 16, 16), 16)
 
-    def scatter(layer):
-        cross = {}
-        for d in FAR + (0,):
-            rows = chunk_rows(lax.rem(a2 + d, N))
-            cross[d] = send(
-                cs.at[layer, rows, :],
-                cr.at[layer, rows, :],
-                co_s.at[layer, d],
-                co_r.at[layer, d],
-                sibling,
-            )
-            cross[d].start()
-        pending = list(cross.values())
-        first = {}
-        for d in FAR + (0,):
-            rows = chunk_rows(lax.rem(a1 + d, N))
-            cross[d].wait_recv()
+    def scatter(layer, batch, cross):
+        sent = {}
+        for q, d in enumerate(BATCHES[batch]):
+            rows = pl.ds(64 * batch + 16 * q, 16)
+            cross[q].wait_recv()
             value = of[rows, :] + cr[layer, rows, :].astype(F32)
+            s1[layer, rows, :] = value.astype(BF16)
             if d:
-                s1[layer, rows, :] = value.astype(BF16)
-                first[d] = send(
+                sent[d] = send(
                     s1.at[layer, rows, :],
                     r1.at[layer, d],
                     r1_s.at[layer, d],
                     r1_r.at[layer, d],
-                    peer1(d),
+                    peer1(N - d),
                 )
-                first[d].start()
-        total = value
-        for d in NEAR:
+                sent[d].start()
+            else:
+                r1[layer, 0] = value.astype(BF16)
+        return sent
+
+    def collect(layer, first):
+        total = r1[layer, 0].astype(F32)
+        for d in FAR:
             first[d].wait_recv()
             total = total + r1[layer, d].astype(F32)
-        pending += first.values()
         total = total.astype(BF16)
         stacked = jnp.concatenate(
             [total[:, KC * k : KC * k + KC] for k in range(CHUNKS)] + [jnp.zeros((16, KC), BF16)],
@@ -372,61 +382,56 @@
         for d in NEAR:
             second[d].wait_recv()
             total = total + r2[layer, d].astype(F32)
-        pending += second.values()
-        return total, pending
-
-    def layer_of(layer, block, side, px, rx, w_in, w_out, prepare, loads_in, loads_out):
-        first = gather(layer, block, side)
-        prepare()
-        pending, forwards = spread(layer, first)
+        return total, second
+
+    def layer_of(layer, block, side, px, rx, w_in, w_out, loads_in, loads_out):
+        first, second, forwards = gather(layer, block, side)
+        receive(layer, 0, second, forwards)
         for load in loads_in:
             load.wait()
-        if layer == 0:
-            cw[half_rows(0), :] = jnp.dot(
-                xm[half_rows(0), DL:], selector, preferred_element_type=F32
-            )
         x0 = project(layer, 0, px, rx, w_in)
-        rest(layer, forwards)
+        receive(layer, 1, second, forwards)
         x1 = project(layer, 1, px, rx, w_in)
-        if layer == 0:
-            cw[half_rows(1), :] = jnp.dot(
-                xm[half_rows(1), DL:], selector, preferred_element_type=F32
-            )
         h0 = activate(layer, 0, px, rx, x0)
         h1 = activate(layer, 1, px, rx, x1)
         for load in loads_out:
             load.wait()
-        lower(layer, w_out, (h0, h1))
-        total, more = scatter(layer)
-        return total, pending + x0 + x1 + h0 + h1 + more
+        c0 = lower(layer, 0, w_out, h0)
+        sent = scatter(layer, 0, c0)
+        c1 = lower(layer, 1, w_out, h1)
+        sent.update(scatter(layer, 1, c1))
+        total, last = collect(layer, sent)
+        started = first + x0 + x1 + h0 + h1 + c0 + c1
+        for group in (second, forwards, sent, last):
+            started += group.values()
+        return total, started
 
     expert = dp // (EH // 256)
     at = iota((KC, 128), 0)
     selector = ((at == expert) | (at == expert + EXPERTS)).astype(F32).astype(BF16)
 
-    def prepare():
-        to = iota((128, 128), 0)
-        source = lax.rem(to // 2, 8) * 16 + (to // 16) * 2 + lax.rem(to, 2)
-        perm[...] = (source == iota((128, 128), 1)).astype(F32).astype(BF16)
-        side_row = iota((KC, 128), 0)
-        side_lane = iota((KC, 128), 1)
-        is_part = (side_row >= 32) & (side_row < 35)
-        w1[:256, DL:] = jnp.zeros((256, KC), BF16)
-        w1[272:320, :DL] = jnp.zeros((48, DL), BF16)
-        w1[336:, :DL] = jnp.zeros((48, DL), BF16)
-        to_row = iota((128, KC), 0)
-        to_lane = iota((128, KC), 1)
-        wanted = (to_lane >= 32) & (to_lane < 35) & (to_row == to_lane + 64)
-        w1[256:, DL:] = wanted.astype(F32).astype(BF16)
-        w2[144:, :] = jnp.zeros((112, DL), BF16)
-        w3[DL:, :512] = jnp.zeros((KC, 512), BF16)
-        w3[:DL, 512:] = jnp.zeros((DL, 128), BF16)
-        w3[DL:, 512:] = (is_part & (side_lane == side_row - 32)).astype(F32).astype(BF16)
+    to = iota((128, 128), 0)
+    source = lax.rem(to // 2, 8) * 16 + (to // 16) * 2 + lax.rem(to, 2)
+    perm[...] = (source == iota((128, 128), 1)).astype(F32).astype(BF16)
+    side_row = iota((KC, 128), 0)
+    side_lane = iota((KC, 128), 1)
+    is_part = (side_row >= 32) & (side_row < 35)
+    w1[:256, DL:] = jnp.zeros((256, KC), BF16)
+    w1[272:320, :DL] = jnp.zeros((48, DL), BF16)
+    w1[336:, :DL] = jnp.zeros((48, DL), BF16)
+    to_row = iota((128, KC), 0)
+    to_lane = iota((128, KC), 1)
+    wanted = (to_lane >= 32) & (to_lane < 35) & (to_row == to_lane + 64)
+    w1[256:, DL:] = wanted.astype(F32).astype(BF16)
+    w2[144:, :] = jnp.zeros((112, DL), BF16)
+    w3[DL:, :512] = jnp.zeros((KC, 512), BF16)
+    w3[:DL, 512:] = jnp.zeros((DL, 128), BF16)
+    w3[DL:, 512:] = (is_part & (side_lane == side_row - 32)).astype(F32).astype(BF16)
 
     tokens_block = tb[...]
     side = jnp.where(row >= 14, ab[...] + sums_of_squares(tokens_block), 0.0)
     dense, pending = layer_of(
-        0, tokens_block, side, px0, rx0, w1, w2, prepare, loads[0:4], loads[4:5]
+        0, tokens_block, side, px0, rx0, w1, w2, loads[0:4], loads[4:5]
     )
     fill_gain(gain2)
     mixed = rounded(tb[...] + dense)
@@ -434,7 +439,7 @@
     tb[...] = mixed
     side = jnp.where(row >= 14, sums_of_squares(mixed), 0.0)
     routed, more = layer_of(
-        1, mixed, side, px1, rx1, w3, w4, lambda: None, loads[5:7], loads[7:]
+        1, mixed, side, px1, rx1, w3, w4, loads[5:7], loads[7:]
     )
     tb[...] = tb[...] + routed
     live = iota((2, KC), 0) < newt[0]

time: 96.7 us -> 91.7 us (0.948)
  Pallas kernels: 94.5 us -> 89.5 us
    pallas_call x1, Pallas kernels: 94.5 us -> 89.5 us  [shards(): pl.pallas_call(kernel, out_shape=jax.ShapeDtypeStruct((2, DL), F32), in_s...]
where the time goes in v3:
time: 91.7 us; the launch traced here: 91.5 us
  Pallas kernels  89.5 us (98%)
  other arithmetic  1.31 us (1%)
    pallas_call x1, Pallas kernels, shards(): pl.pallas_call(kernel, out_shape=jax.ShapeDtypeStruct((2, DL), F32), in_s...  89.5 us

profile of v3, /device:TPU:1, one launch (start us, length us, event | category | flops | bytes accessed | tf_op | source)
XLA Modules:
  0.0 91.5 jit_solution(6192852793493998996)
XLA Ops:
  0.7 89.5 %layers.1 = f32[2,1792]{1,0:T(2,128)} custom-call(bf16[2,1792]{1,0:T(2,128)(2,1)} %tok.1, s32[1]{0:T(128)S(6)} %copy.13.newt, f32[1792]{0:T(1024)} %gain1.1, bf16[144,1792]{1,0:T(8,128)(2,1)} %bitcast.2, bf16[144,1792]{1,0:T(8,128)(2,1)} %bitcast.3, bf16[144,1792]{1,0:T(8,128)(2,1)} %down.1, f32[1792]{0:T(1024)} %gain2.1, s32[2,8]{1,0:T(2,128)} %ids.1, ...), custom_call_target="tpu_custom_call" | custom-call | tf_op jit(solution)/shard_map/layers/pallas_call | solution.py:470
  90.2 1.3 %convert_element_type.3 = bf16[2,1792]{1,0:T(2,128)(2,1)} convert(f32[2,1792]{1,0:T(2,128)} %layers.1) | non-fusion elementwise | flops 3584 | bytes 21504 | tf_op jit(solution)/shard_map/convert_element_type | solution.py:548

commit v4 on v3

--- a/solution.py
+++ b/solution.py
@@ -17,13 +17,18 @@
 KC = 256
 CHUNKS = DL // KC
 HALF = 128
-XR = HALF // NX
 MESH = pl.DeviceIdType.MESH
 F32 = jnp.float32
 BF16 = jnp.bfloat16
 FAR = (4, 3, 5, 2, 6, 1, 7)
 NEAR = (1, 7, 2, 6, 3, 5, 4)
-BATCHES = ((3, 5, 4, 0), (1, 7, 2, 6))
+BATCHES = ((4, 3, 5, 0), (2, 6, 1, 7))
+FIRST = (4, 3, 5)
+LATER = (2, 6, 1, 7)
+EARLY = 1
+STEPS = ("r0", "r1", "a0", "a1", "l0", "s0", "l1", "s1")
+START = tuple(sum(len(b) for b in BATCHES[:i]) for i in range(len(BATCHES)))
+XR = tuple(8 * len(b) for b in BATCHES)
 
 
 def iota(shape, dim):
@@ -35,19 +40,24 @@
 
 
 def kernel(
-    tok,
+    tok_in,
     newt,
-    gain1,
+    gain1_in,
     gate,
     up,
     down,
-    gain2,
-    ids,
-    wts,
+    gain2_in,
+    ids_in,
+    wts_in,
     egate,
     eup,
     edown,
     out,
+    tok,
+    gain1,
+    gain2,
+    ids,
+    wts,
     w1,
     w2,
     w3,
@@ -71,6 +81,7 @@
     r1,
     s2,
     r2,
+    ssem,
     wsem,
     ag1_s,
     ag1_r,
@@ -129,6 +140,20 @@
         pl.semaphore_signal(barrier, inc=1, device_id=peerx(d), device_id_type=MESH)
     pl.semaphore_signal(barrier, inc=1, device_id=sibling, device_id_type=MESH)
 
+    small = [
+        pltpu.make_async_copy(src, dst, ssem.at[i])
+        for i, (src, dst) in enumerate(
+            (
+                (tok_in, tok),
+                (gain1_in, gain1),
+                (ids_in, ids),
+                (wts_in, wts),
+                (gain2_in, gain2),
+            )
+        )
+    ]
+    for load in small:
+        load.start()
     loads = [
         pltpu.make_async_copy(src, dst, wsem.at[i])
         for i, (src, dst) in enumerate(
@@ -169,6 +194,8 @@
         for k in range(CHUNKS):
             gb[2 * k : 2 * k + 2, :] = jnp.broadcast_to(gain[KC * k : KC * k + KC][None, :], (2, KC))
 
+    for load in small:
+        load.wait()
     stream = tok[...].astype(F32)
     tb[...] = jnp.zeros((16, KC), F32)
     for k in range(CHUNKS):
@@ -186,7 +213,7 @@
         lane2 < EXPERTS, high, jnp.where(lane2 < 2 * EXPERTS, combine - high, 0.0)
     )
 
-    def gather(layer, block, side):
+    def gather(layer, block, side, earlier):
         place_rows = chunk_rows(a2)
         mine = gath.at[layer, 0, place_rows, :]
         gath[layer, 0, place_rows, :] = jnp.where(
@@ -199,15 +226,39 @@
         ]
         for copy in first:
             copy.start()
-        for copy in first:
+        line = gath.at[layer, 0]
+        second = {
+            d: send(line, gath.at[layer, d], ag2_s.at[layer, d], ag2_r.at[layer, d], peer1(d))
+            for d in FAR
+        }
+
+        def pass_on(rows, offsets):
+            for d in offsets:
+                send(
+                    gath.at[layer, 0, rows, :],
+                    gath.at[layer, d, rows, :],
+                    ag2_s.at[layer, d],
+                    ag2_r.at[layer, d],
+                    peer1(d),
+                ).start()
+
+        pass_on(place_rows, FIRST + LATER)
+        if layer == 0:
+            fill()
+        else:
+            for copy in earlier:
+                copy.wait_send()
+        held = []
+        for i, copy in enumerate(reversed(first)):
             copy.wait_recv()
-        line = gath.at[layer, 0]
-        second = {}
-        for d in FAR:
-            second[d] = send(
-                line, gath.at[layer, d], ag2_s.at[layer, d], ag2_r.at[layer, d], peer1(d)
-            )
-            second[d].start()
+            rows = chunk_rows(lax.rem(a2 + N - FAR[N - 2 - i], N))
+            pass_on(rows, FIRST)
+            if i + 1 < EARLY:
+                pass_on(rows, LATER)
+            else:
+                held.append(rows)
+        for rows in held:
+            pass_on(rows, LATER)
         forwards = {0: forward(layer, 0)}
         return first, second, forwards
 
@@ -228,7 +279,7 @@
             perm[...], jnp.concatenate(groups, axis=1), preferred_element_type=F32
         ).astype(BF16)
         for q in range(len(groups)):
-            start = HALF * batch + 64 * other + 16 * q
+            start = 32 * START[batch] + 16 * len(groups) * other + 16 * q
             for k in range(CHUNKS + 1):
                 xm[start : start + 16, KC * k : KC * k + KC] = moved[
                     16 * k : 16 * k + 16, KC * q : KC * q + KC
@@ -245,10 +296,15 @@
         permuted(layer, batch, 1)
 
     def part_rows(batch, index):
-        return pl.ds(pl.multiple_of(batch * HALF + index * XR, XR), XR)
+        return pl.ds(
+            pl.multiple_of(32 * START[batch] + index * XR[batch], XR[batch]), XR[batch]
+        )
+
+    def batch_rows(batch):
+        return pl.ds(32 * START[batch], 32 * len(BATCHES[batch]))
 
     def project(layer, batch, px, rx, weight):
-        rows = pl.ds(batch * HALF, HALF)
+        rows = batch_rows(batch)
         px[rows, :] = lax.dot_general(
             xm[rows, :],
             weight[...],
@@ -258,7 +314,7 @@
         copies = [
             send(
                 px.at[part_rows(batch, lax.rem(x + d, NX)), :],
-                rx.at[batch, d],
+                rx.at[d, pl.ds(8 * START[batch], XR[batch]), :],
                 rx_s.at[layer, batch, d],
                 rx_r.at[layer, batch, d],
                 peerx(d),
@@ -276,9 +332,9 @@
         total = px[rows, :].astype(F32)
         for copy, d in zip(copies, (2, 1, 3)):
             copy.wait_recv()
-            total = total + rx[batch, d].astype(F32)
+            total = total + rx[d, pl.ds(8 * START[batch], XR[batch]), :].astype(F32)
         tail = total[:, total.shape[1] - 128 :]
-        spot = iota((XR, 128), 1)
+        spot = iota((XR[batch], 128), 1)
         if layer == 0:
             used = (spot >= 96) & (spot < 99)
         else:
@@ -313,15 +369,16 @@
     def lower(layer, batch, weight, copies):
         for copy in copies:
             copy.wait_recv()
-        value = hid[layer, HALF * batch : HALF * batch + HALF, :]
-        rows = pl.ds(64 * batch, 64)
+        value = hid[layer, batch_rows(batch), :]
+        count = 16 * len(BATCHES[batch])
+        rows = pl.ds(16 * START[batch], count)
         for k in range(CHUNKS):
             part = jnp.dot(value, weight[:, KC * k : KC * k + KC], preferred_element_type=F32)
-            of[rows, KC * k : KC * k + KC] = part[:64, :]
-            cs[layer, rows, KC * k : KC * k + KC] = part[64:, :].astype(BF16)
+            of[rows, KC * k : KC * k + KC] = part[:count, :]
+            cs[layer, rows, KC * k : KC * k + KC] = part[count:, :].astype(BF16)
         cross = []
         for q, d in enumerate(BATCHES[batch]):
-            part_of = pl.ds(64 * batch + 16 * q, 16)
+            part_of = pl.ds(16 * START[batch] + 16 * q, 16)
             cross.append(
                 send(
                     cs.at[layer, part_of, :],
@@ -340,7 +397,7 @@
     def scatter(layer, batch, cross):
         sent = {}
         for q, d in enumerate(BATCHES[batch]):
-            rows = pl.ds(64 * batch + 16 * q, 16)
+            rows = pl.ds(16 * START[batch] + 16 * q, 16)
             cross[q].wait_recv()
             value = of[rows, :] + cr[layer, rows, :].astype(F32)
             s1[layer, rows, :] = value.astype(BF16)
@@ -357,7 +414,7 @@
                 r1[layer, 0] = value.astype(BF16)
         return sent
 
-    def collect(layer, first):
+    def collect(layer, first, started):
         total = r1[layer, 0].astype(F32)
         for d in FAR:
             first[d].wait_recv()
@@ -378,60 +435,70 @@
                 peer2(d),
             )
             second[d].start()
+        for copy in started:
+            copy.wait_send()
         total = s2[layer, chunk_rows(a2), :].astype(F32)
         for d in NEAR:
             second[d].wait_recv()
             total = total + r2[layer, d].astype(F32)
-        return total, second
-
-    def layer_of(layer, block, side, px, rx, w_in, w_out, loads_in, loads_out):
-        first, second, forwards = gather(layer, block, side)
-        receive(layer, 0, second, forwards)
-        for load in loads_in:
-            load.wait()
-        x0 = project(layer, 0, px, rx, w_in)
-        receive(layer, 1, second, forwards)
-        x1 = project(layer, 1, px, rx, w_in)
-        h0 = activate(layer, 0, px, rx, x0)
-        h1 = activate(layer, 1, px, rx, x1)
-        for load in loads_out:
-            load.wait()
-        c0 = lower(layer, 0, w_out, h0)
-        sent = scatter(layer, 0, c0)
-        c1 = lower(layer, 1, w_out, h1)
-        sent.update(scatter(layer, 1, c1))
-        total, last = collect(layer, sent)
-        started = first + x0 + x1 + h0 + h1 + c0 + c1
-        for group in (second, forwards, sent, last):
+        return total, list(second.values())
+
+    def layer_of(layer, block, side, px, rx, w_in, w_out, loads_in, loads_out, earlier):
+        first, second, forwards = gather(layer, block, side, earlier)
+        parts, hiddens, crossed, sent = {}, {}, {}, {}
+        for step in STEPS:
+            b = int(step[1])
+            if step == "r0":
+                receive(layer, b, second, forwards)
+                for load in loads_in:
+                    load.wait()
+                parts[b] = project(layer, b, px, rx, w_in)
+            elif step[0] == "r":
+                receive(layer, b, second, forwards)
+                parts[b] = project(layer, b, px, rx, w_in)
+            elif step[0] == "a":
+                hiddens[b] = activate(layer, b, px, rx, parts[b])
+            elif step[0] == "l":
+                if b == 0:
+                    for load in loads_out:
+                        load.wait()
+                crossed[b] = lower(layer, b, w_out, hiddens[b])
+            else:
+                sent.update(scatter(layer, b, crossed[b]))
+        started = list(first)
+        for group in (parts, hiddens, crossed):
+            started += [copy for copies in group.values() for copy in copies]
+        for group in (second, forwards, sent):
             started += group.values()
-        return total, started
+        return collect(layer, sent, started)
 
     expert = dp // (EH // 256)
     at = iota((KC, 128), 0)
     selector = ((at == expert) | (at == expert + EXPERTS)).astype(F32).astype(BF16)
 
-    to = iota((128, 128), 0)
-    source = lax.rem(to // 2, 8) * 16 + (to // 16) * 2 + lax.rem(to, 2)
-    perm[...] = (source == iota((128, 128), 1)).astype(F32).astype(BF16)
-    side_row = iota((KC, 128), 0)
-    side_lane = iota((KC, 128), 1)
-    is_part = (side_row >= 32) & (side_row < 35)
-    w1[:256, DL:] = jnp.zeros((256, KC), BF16)
-    w1[272:320, :DL] = jnp.zeros((48, DL), BF16)
-    w1[336:, :DL] = jnp.zeros((48, DL), BF16)
-    to_row = iota((128, KC), 0)
-    to_lane = iota((128, KC), 1)
-    wanted = (to_lane >= 32) & (to_lane < 35) & (to_row == to_lane + 64)
-    w1[256:, DL:] = wanted.astype(F32).astype(BF16)
-    w2[144:, :] = jnp.zeros((112, DL), BF16)
-    w3[DL:, :512] = jnp.zeros((KC, 512), BF16)
-    w3[:DL, 512:] = jnp.zeros((DL, 128), BF16)
-    w3[DL:, 512:] = (is_part & (side_lane == side_row - 32)).astype(F32).astype(BF16)
+    def fill():
+        to = iota((128, 128), 0)
+        source = lax.rem(to // 2, 8) * 16 + (to // 16) * 2 + lax.rem(to, 2)
+        perm[...] = (source == iota((128, 128), 1)).astype(F32).astype(BF16)
+        side_row = iota((KC, 128), 0)
+        side_lane = iota((KC, 128), 1)
+        is_part = (side_row >= 32) & (side_row < 35)
+        w1[:256, DL:] = jnp.zeros((256, KC), BF16)
+        w1[272:320, :DL] = jnp.zeros((48, DL), BF16)
+        w1[336:, :DL] = jnp.zeros((48, DL), BF16)
+        to_row = iota((128, KC), 0)
+        to_lane = iota((128, KC), 1)
+        wanted = (to_lane >= 32) & (to_lane < 35) & (to_row == to_lane + 64)
+        w1[256:, DL:] = wanted.astype(F32).astype(BF16)
+        w2[144:, :] = jnp.zeros((112, DL), BF16)
+        w3[DL:, :512] = jnp.zeros((KC, 512), BF16)
+        w3[:DL, 512:] = jnp.zeros((DL, 128), BF16)
+        w3[DL:, 512:] = (is_part & (side_lane == side_row - 32)).astype(F32).astype(BF16)
 
     tokens_block = tb[...]
     side = jnp.where(row >= 14, ab[...] + sums_of_squares(tokens_block), 0.0)
     dense, pending = layer_of(
-        0, tokens_block, side, px0, rx0, w1, w2, loads[0:4], loads[4:5]
+        0, tokens_block, side, px0, rx0, w1, w2, loads[0:4], loads[4:5], ()
     )
     fill_gain(gain2)
     mixed = rounded(tb[...] + dense)
@@ -439,13 +506,13 @@
     tb[...] = mixed
     side = jnp.where(row >= 14, sums_of_squares(mixed), 0.0)
     routed, more = layer_of(
-        1, mixed, side, px1, rx1, w3, w4, loads[5:7], loads[7:]
+        1, mixed, side, px1, rx1, w3, w4, loads[5:7], loads[7:], pending
     )
     tb[...] = tb[...] + routed
     live = iota((2, KC), 0) < newt[0]
     for k in range(CHUNKS):
         out[:, KC * k : KC * k + KC] = jnp.where(live, tb[2 * k : 2 * k + 2, :], 0.0)
-    for copy in pending + more:
+    for copy in more:
         copy.wait_send()
 
 
@@ -470,22 +537,14 @@
     result = pl.pallas_call(
         kernel,
         out_shape=jax.ShapeDtypeStruct((2, DL), F32),
-        in_specs=[
-            vmem,
-            smem,
-            vmem,
-            anywhere,
-            anywhere,
-            anywhere,
-            vmem,
-            vmem,
-            vmem,
-            anywhere,
-            anywhere,
-            anywhere,
-        ],
+        in_specs=[anywhere, smem] + [anywhere] * 10,
         out_specs=vmem,
         scratch_shapes=[
+            pltpu.VMEM((2, DL), BF16),
+            pltpu.VMEM((DL,), F32),
+            pltpu.VMEM((DL,), F32),
+            pltpu.VMEM((2, TOP), jnp.int32),
+            pltpu.VMEM((2, TOP), F32),
             pltpu.VMEM((384, DL + KC), BF16),
             pltpu.VMEM((256, DL), BF16),
             pltpu.VMEM((DL + KC, 640), BF16),
@@ -499,8 +558,8 @@
             pltpu.VMEM((2 * HALF, 128), F32),
             pltpu.VMEM((2 * HALF, 384), BF16),
             pltpu.VMEM((2 * HALF, 640), BF16),
-            pltpu.VMEM((2, NX, XR, 384), BF16),
-            pltpu.VMEM((2, NX, XR, 640), BF16),
+            pltpu.VMEM((NX, 64, 384), BF16),
+            pltpu.VMEM((NX, 64, 640), BF16),
             pltpu.VMEM((2, 2 * HALF, 256), BF16),
             pltpu.VMEM((2, HALF, DL), BF16),
             pltpu.VMEM((2, HALF, DL), BF16),
@@ -509,6 +568,7 @@
             pltpu.VMEM((2, N, 16, DL), BF16),
             pltpu.VMEM((2, 128, KC), BF16),
             pltpu.VMEM((2, N, 16, KC), BF16),
+            sems((5,)),
             sems((8,)),
             sems((2, N)),
             sems((2, N)),
@@ -516,10 +576,10 @@
             sems((2, N)),
             sems((2, N)),
             sems((2, N)),
-            sems((2, 2, NX)),
-            sems((2, 2, NX)),
-            sems((2, 2, NX)),
-            sems((2, 2, NX)),
+            sems((2, len(BATCHES), NX)),
+            sems((2, len(BATCHES), NX)),
+            sems((2, len(BATCHES), NX)),
+            sems((2, len(BATCHES), NX)),
             sems((2, N)),
             sems((2, N)),
             sems((2, N)),

time: 91.7 us -> 86.7 us (0.945)
  Pallas kernels: 89.5 us -> 84.5 us
    pallas_call x1, Pallas kernels: 89.5 us -> 84.5 us  [shards(): pl.pallas_call(kernel, out_shape=jax.ShapeDtypeStruct((2, DL), F32), in_s...]
where the time goes in v4:
time: 86.7 us; the launch traced here: 86.5 us
  Pallas kernels  84.5 us (97%)
  other arithmetic  1.31 us (2%)
    pallas_call x1, Pallas kernels, shards(): pl.pallas_call(kernel, out_shape=jax.ShapeDtypeStruct((2, DL), F32), in_s...  84.5 us

profile of v4, /device:TPU:1, one launch (start us, length us, event | category | flops | bytes accessed | tf_op | source)
XLA Modules:
  0.0 86.5 jit_solution(16780523302738158048)
XLA Ops:
  0.7 84.5 %layers.1 = f32[2,1792]{1,0:T(2,128)} custom-call(bf16[2,1792]{1,0:T(2,128)(2,1)} %tok_in.1, s32[1]{0:T(128)S(6)} %copy.13.newt, f32[1792]{0:T(1024)} %gain1_in.1, bf16[144,1792]{1,0:T(8,128)(2,1)} %bitcast.2, bf16[144,1792]{1,0:T(8,128)(2,1)} %bitcast.3, bf16[144,1792]{1,0:T(8,128)(2,1)} %down.1, f32[1792]{0:T(1024)} %gain2_in.1, s32[2,8]{1,0:T(2,128)} %ids_in.1, ...), custom_call_target="tpu_custom_call" | custom-call | tf_op jit(solution)/shard_map/layers/pallas_call | solution.py:537
  85.2 1.3 %convert_element_type.3 = bf16[2,1792]{1,0:T(2,128)(2,1)} convert(f32[2,1792]{1,0:T(2,128)} %layers.1) | non-fusion elementwise | flops 3584 | bytes 21504 | tf_op jit(solution)/shard_map/convert_element_type | solution.py:608

commit v5 on v4

--- a/solution.py
+++ b/solution.py
@@ -189,10 +189,10 @@
             lane == 32, high, jnp.where(lane == 33, middle, jnp.where(lane == 34, low, 0.0))
         )
 
-    def fill_gain(gain):
-        gb[...] = jnp.zeros((16, KC), F32)
+    def fill_gain(layer, gain):
+        gb[layer] = jnp.zeros((16, KC), F32)
         for k in range(CHUNKS):
-            gb[2 * k : 2 * k + 2, :] = jnp.broadcast_to(gain[KC * k : KC * k + KC][None, :], (2, KC))
+            gb[layer, 2 * k : 2 * k + 2, :] = jnp.broadcast_to(gain[KC * k : KC * k + KC][None, :], (2, KC))
 
     for load in small:
         load.wait()
@@ -200,7 +200,7 @@
     tb[...] = jnp.zeros((16, KC), F32)
     for k in range(CHUNKS):
         tb[2 * k : 2 * k + 2, :] = stream[:, KC * k : KC * k + KC]
-    fill_gain(gain1)
+    fill_gain(0, gain1)
     lane2 = iota((2, KC), 1)
     combine = jnp.zeros((2, KC), F32)
     chosen = ids[...]
@@ -217,7 +217,7 @@
         place_rows = chunk_rows(a2)
         mine = gath.at[layer, 0, place_rows, :]
         gath[layer, 0, place_rows, :] = jnp.where(
-            row < 2 * CHUNKS, block * gb[...], side
+            row < 2 * CHUNKS, block * gb[layer], side
         ).astype(BF16)
         if layer == 0:
             pl.semaphore_wait(barrier, 2 * (N - 1) + NX)
@@ -373,9 +373,10 @@
         count = 16 * len(BATCHES[batch])
         rows = pl.ds(16 * START[batch], count)
         for k in range(CHUNKS):
-            part = jnp.dot(value, weight[:, KC * k : KC * k + KC], preferred_element_type=F32)
-            of[rows, KC * k : KC * k + KC] = part[:count, :]
-            cs[layer, rows, KC * k : KC * k + KC] = part[count:, :].astype(BF16)
+            part = jnp.dot(
+                value[count:, :], weight[:, KC * k : KC * k + KC], preferred_element_type=F32
+            )
+            cs[layer, rows, KC * k : KC * k + KC] = part.astype(BF16)
         cross = []
         for q, d in enumerate(BATCHES[batch]):
             part_of = pl.ds(16 * START[batch] + 16 * q, 16)
@@ -389,6 +390,10 @@
                 )
             )
             cross[q].start()
+        for k in range(CHUNKS):
+            of[rows, KC * k : KC * k + KC] = jnp.dot(
+                value[:count, :], weight[:, KC * k : KC * k + KC], preferred_element_type=F32
+            )
         return cross
 
     def chunk_rows(index):
@@ -477,6 +482,7 @@
     selector = ((at == expert) | (at == expert + EXPERTS)).astype(F32).astype(BF16)
 
     def fill():
+        fill_gain(1, gain2)
         to = iota((128, 128), 0)
         source = lax.rem(to // 2, 8) * 16 + (to // 16) * 2 + lax.rem(to, 2)
         perm[...] = (source == iota((128, 128), 1)).astype(F32).astype(BF16)
@@ -500,7 +506,6 @@
     dense, pending = layer_of(
         0, tokens_block, side, px0, rx0, w1, w2, loads[0:4], loads[4:5], ()
     )
-    fill_gain(gain2)
     mixed = rounded(tb[...] + dense)
     mixed = jnp.where(row < 2 * CHUNKS, mixed, 0.0)
     tb[...] = mixed
@@ -550,7 +555,7 @@
             pltpu.VMEM((DL + KC, 640), BF16),
             pltpu.VMEM((256, DL), BF16),
             pltpu.VMEM((16, KC), F32),
-            pltpu.VMEM((16, KC), F32),
+            pltpu.VMEM((2, 16, KC), F32),
             pltpu.VMEM((16, KC), F32),
             pltpu.VMEM((128, 128), BF16),
             pltpu.VMEM((2, 2 * N, 128, KC), BF16),

time: 86.7 us -> 86.6 us (level)
  no operation moved by 1% of the time
where the time goes in v5:
time: 86.6 us; the launch traced here: 86.4 us
  Pallas kernels  84.4 us (97%)
  other arithmetic  1.31 us (2%)
    pallas_call x1, Pallas kernels, shards(): pl.pallas_call(kernel, out_shape=jax.ShapeDtypeStruct((2, DL), F32), in_s...  84.4 us

profile of v5, /device:TPU:1, one launch (start us, length us, event | category | flops | bytes accessed | tf_op | source)
XLA Modules:
  0.0 86.4 jit_solution(13342464762602085480)
XLA Ops:
  0.7 84.4 %layers.1 = f32[2,1792]{1,0:T(2,128)} custom-call(bf16[2,1792]{1,0:T(2,128)(2,1)} %tok_in.1, s32[1]{0:T(128)S(6)} %copy.13.newt, f32[1792]{0:T(1024)} %gain1_in.1, bf16[144,1792]{1,0:T(8,128)(2,1)} %bitcast.2, bf16[144,1792]{1,0:T(8,128)(2,1)} %bitcast.3, bf16[144,1792]{1,0:T(8,128)(2,1)} %down.1, f32[1792]{0:T(1024)} %gain2_in.1, s32[2,8]{1,0:T(2,128)} %ids_in.1, ...), custom_call_target="tpu_custom_call" | custom-call | tf_op jit(solution)/shard_map/layers/pallas_call | solution.py:542
  85.1 1.3 %convert_element_type.3 = bf16[2,1792]{1,0:T(2,128)(2,1)} convert(f32[2,1792]{1,0:T(2,128)} %layers.1) | non-fusion elementwise | flops 3584 | bytes 21504 | tf_op jit(solution)/shard_map/convert_element_type | solution.py:613
